TPU v7x, 32 devices: a whole 2x2x4 slice. The times are simulated.
32 devices in a mesh: seq: 16 (over z, y, x), head: 2 (over core).
Axes of the slice: x: 2, y: 2, z: 4, core: 2. Of those that a mesh axis runs over, the one named last changes fastest.
Arguments:
- q_lin: bfloat16 [4096, 512], P('seq', 'head'), may hold values from -6 to 6
- k_lin: bfloat16 [4096, 512], P('seq', 'head'), may hold values from -6 to 6
- v_lin: bfloat16 [4096, 512], P('seq', 'head'), may hold values from -6 to 6
- log_decay: float32 [4, 4096], P('head', 'seq'), may hold values from -0.4 to 0, as said below
- q_soft: bfloat16 [4096, 512], P('seq', 'head'), may hold values from -12 to 12
- k_soft: bfloat16 [4096, 512], P('seq', 'head'), may hold values from -6 to 6
- v_soft: bfloat16 [4096, 512], P('seq', 'head'), may hold values from -6 to 6
- wo_lin: bfloat16 [512, 4096], P('head'), may hold values from -0.375 to 0.375
- wo_soft: bfloat16 [512, 4096], P('head'), may hold values from -0.375 to 0.375
Outputs:
- lin_mixed: bfloat16 [4096, 4096], P('seq', 'head')
- soft_mixed: bfloat16 [4096, 4096], P('seq', 'head')
Inputs may be any that keep to these rules, and one draw needn't show every extreme that they name: `log_decay`: log decays are never positive.
All inputs are finite; a program needn't handle non-finite values.
Results may differ from a plain program's by a relative error of at most 0.012.
Values may be sent and summed in bfloat16 or wider, within the bound.
A program may use at most 64 MiB of HBM per device.

v0:
```python
import math
import jax
import jax.numpy as jnp
from jax import lax
from jax.sharding import PartitionSpec as P

HIGHEST = lax.Precision.HIGHEST
NEG_BIG = -1e30


def prefix(shard, axis, combine, identity):
    size, here = (lax.axis_size(axis), lax.axis_index(axis))
    everything = jax.tree.map(
        lambda part, kind: lax.all_gather(part.astype(kind), axis),
        shard,
        (jnp.bfloat16, jnp.bfloat16),
    )
    start = jax.tree.map(
        lambda part, zero: jnp.broadcast_to(jnp.asarray(zero, part.dtype), part.shape),
        shard,
        identity,
    )

    def turn(k, before):
        reached = k < here
        new = combine(
            before, jax.tree.map(lambda part, own: part[k].astype(own.dtype), everything, shard)
        )
        return jax.tree.map(lambda a, b: jnp.where(reached, a, b), new, before)

    return lax.fori_loop(0, size, turn, start)


def second_half(device):
    return 2 * device + 1


def absorb(state, query_half, key_block, value_block, allowed, factor):
    row_top, row_sum, weighted = state
    scores = (
        jnp.einsum("qhd,khd->hqk", query_half, key_block, preferred_element_type=jnp.float32)
        * factor
    )
    if allowed is not None:
        scores = jnp.where(allowed[None], scores, -jnp.inf)
    new_top = jnp.maximum(row_top, jnp.max(scores, axis=-1))
    shrink = jnp.exp(row_top - new_top)
    weights = jnp.exp(scores - new_top[:, :, None])
    row_sum = row_sum * shrink + jnp.sum(weights, axis=-1)
    weighted = weighted * shrink.T[:, :, None] + jnp.einsum(
        "hqk,khd->qhd",
        weights.astype(jnp.bfloat16),
        value_block,
        preferred_element_type=jnp.float32,
    )
    return (new_top, row_sum, weighted)


def lightning_heads(q_lin, k_lin, v_lin, log_decay):
    row_count = q_lin.shape[0]
    head_count = log_decay.shape[0]
    head_width = q_lin.shape[1] // head_count
    query_plain = q_lin.reshape(row_count, head_count, head_width)
    key_plain = k_lin.reshape(row_count, head_count, head_width)
    queries = query_plain.astype(jnp.float32)
    key_rows = key_plain.astype(jnp.float32)
    values = v_lin.astype(jnp.float32).reshape(row_count, head_count, head_width)
    cumulative = jnp.cumsum(log_decay, axis=1)
    lower = jnp.arange(row_count)[:, None] >= jnp.arange(row_count)[None, :]
    decay_gap = jnp.where(lower[None], cumulative[:, :, None] - cumulative[:, None, :], -jnp.inf)
    scores = jnp.einsum(
        "thd,shd->hts", query_plain, key_plain, preferred_element_type=jnp.float32
    ) * jnp.exp(decay_gap)
    inside = jnp.einsum("hts,shd->thd", scores, values, precision=HIGHEST)
    closing = jnp.exp(cumulative[:, -1:] - cumulative)
    own_state = jnp.einsum(
        "shd,she->hde", key_rows * closing.T[:, :, None], values, precision=HIGHEST
    )
    own_decay = cumulative[:, -1]

    def combine(earlier, later):
        return (jnp.exp(later[1])[:, None, None] * earlier[0] + later[0], earlier[1] + later[1])

    identity = (jnp.zeros_like(own_state), jnp.zeros_like(own_decay))
    carried, _ = prefix((own_state, own_decay), "seq", combine, identity)
    from_before = (
        jnp.einsum("thd,hde->the", queries, carried, precision=HIGHEST)
        * jnp.exp(cumulative).T[:, :, None]
    )
    raw = inside + from_before
    factor = lax.rsqrt(jnp.mean(raw * raw, axis=-1, keepdims=True) + 1e-06)
    return (raw * factor).astype(jnp.bfloat16).reshape(row_count, head_count * head_width)


def softmax_heads(q_soft, k_soft, v_soft, head_width):
    row_count = q_soft.shape[0]
    half_rows = row_count // 2
    head_count = q_soft.shape[1] // head_width
    own_index = lax.axis_index("seq")
    factor = 1.0 / math.sqrt(head_width)
    shaped = q_soft.reshape(2, half_rows, head_count, head_width)
    query_ids = (2 * own_index, second_half(own_index))
    triangle = jnp.arange(half_rows)[:, None] >= jnp.arange(half_rows)[None, :]

    def block_pass(state, side, key_block, value_block, key_id):

        def full_block(inner_state):
            return absorb(inner_state, shaped[side], key_block, value_block, None, factor)

        def diagonal_block(inner_state):
            return absorb(inner_state, shaped[side], key_block, value_block, triangle, factor)

        def skipped(inner_state):
            return inner_state

        def not_below(inner_state):
            return lax.cond(key_id == query_ids[side], diagonal_block, skipped, inner_state)

        return lax.cond(key_id < query_ids[side], full_block, not_below, state)

    start_state = tuple(
        (
            (
                jnp.full((head_count, half_rows), NEG_BIG, jnp.float32),
                jnp.zeros((head_count, half_rows), jnp.float32),
                jnp.zeros((half_rows, head_count, head_width), jnp.float32),
            )
            for side in range(2)
        )
    )
    carry = start_state
    key_piece = lax.all_gather(k_soft, "seq", axis=0, tiled=True)
    value_piece = lax.all_gather(v_soft, "seq", axis=0, tiled=True)
    piece_rows = key_piece.shape[0]
    blocks = piece_rows // half_rows
    key_blocks = key_piece.reshape(blocks, half_rows, head_count, head_width)
    value_blocks = value_piece.reshape(blocks, half_rows, head_count, head_width)
    firsts = half_rows * jnp.arange(blocks, dtype=jnp.int32)

    def inner(state, block_item):
        key_block, value_block, first = block_item
        key_id = first // half_rows
        return (
            tuple(
                (block_pass(state[side], side, key_block, value_block, key_id) for side in range(2))
            ),
            None,
        )

    carry, _ = lax.scan(inner, carry, (key_blocks, value_blocks, firsts))
    halves = [
        (carry[side][2] / carry[side][1].T[:, :, None])
        .astype(jnp.bfloat16)
        .reshape(half_rows, head_count * head_width)
        for side in range(2)
    ]
    return jnp.concatenate(halves, axis=0)


def local(q_lin, k_lin, v_lin, log_decay, q_soft, k_soft, v_soft, wo_lin, wo_soft):
    head_width = q_lin.shape[1] // log_decay.shape[0]
    lin_out = lightning_heads(q_lin, k_lin, v_lin, log_decay)
    soft_out = softmax_heads(q_soft, k_soft, v_soft, head_width)
    lin_term = jnp.dot(lin_out, wo_lin, preferred_element_type=jnp.float32)
    soft_term = jnp.dot(soft_out, wo_soft, preferred_element_type=jnp.float32)
    lin_sum, soft_sum = (
        lax.psum_scatter(
            lin_term.astype(jnp.bfloat16).astype(jnp.float32).astype(jnp.bfloat16),
            "head",
            scatter_dimension=1,
            tiled=True,
        ).astype(jnp.float32),
        lax.psum_scatter(
            soft_term.astype(jnp.bfloat16).astype(jnp.float32).astype(jnp.bfloat16),
            "head",
            scatter_dimension=1,
            tiled=True,
        ).astype(jnp.float32),
    )
    return (lin_sum.astype(jnp.bfloat16), soft_sum.astype(jnp.bfloat16))


def solution(mesh):
    in_specs = (
        P("seq", "head"),
        P("seq", "head"),
        P("seq", "head"),
        P("head", "seq"),
        P("seq", "head"),
        P("seq", "head"),
        P("seq", "head"),
        P("head", None),
        P("head", None),
    )
    out_specs = (P("seq", "head"), P("seq", "head"))
    return jax.shard_map(local, mesh=mesh, in_specs=in_specs, out_specs=out_specs, check_vma=False)
```

profile of v0, /device:TPU:0, one launch (start us, length us, event | category | flops | bytes accessed | tf_op | source)
XLA Modules:
  0.0 389.1 jit_solution(17133437121583700277)
XLA Ops:
  9.3 1.0 copy.69
  10.4 1.8 convolution_convert_fusion.2
  13.8 1.2 dynamic-slice
  15.9 43.7 %all-reduce = bf16[32]{0:T(256)(128)(2,1)S(1)} all-reduce(bf16[32]{0:T(256)(128)(2,1)S(1)} %dynamic-update-slice), channel_id=2, replica_groups=mesh['seq'=16,'head'=2] {'seq'}, use_global_device_ids=true, to_apply=%add | all-reduce | flops 32 | bytes 128
  59.7 1.0 reshape.130
  60.7 1.1 convolution_multiply_fusion.4
  61.8 8.6 %all-gather.10.cloned.1.call-done = bf16[32,128,128]{2,1,0:T(8,128)(2,1)} async-done(((bf16[2,128,128]{2,1,0:T(8,128)(2,1)}), bf16[32,128,128]{2,1,0:T(8,128)(2,1)}) %all-gather.10.cloned.1.call-update) | async-done | bytes 1048592 | tf_op jit(solution)/shard_map/all_gather | solution.py:14
  70.5 15.6 %while.39 = (s32[]{:T(128)}, f32[2,128,128]{2,1,0:T(8,128)S(1)}, s32[]{:T(128)}, bf16[16,2]{1,0:T(8,128)(2,1)S(1)}, bf16[16,2,128,128]{3,2,1,0:T(8,128)(2,1)}, /*index=5*/s32[]{:T(128)}, s32[]{:T(128)}) while((s32[]{:T(128)}, f32[2,128,128]{2,1,0:T(8,128)S(1)}, s32[]{:T(128)}, bf16[16,2]{1,0:T(8,128)(2,1)S(1)}, ...), condition=%wide.region_3.4_spmd.clone, body=%wide.region_2.3_spmd.clone.sunk | while | flops 163846 | bytes 327813 | solution.py:31
  70.5 0.9 fusion.77
  71.5 0.9 fusion.77
  72.4 0.9 fusion.77
  73.4 0.9 fusion.77
  74.4 0.9 fusion.77
  75.4 0.9 fusion.77
  76.3 0.9 fusion.77
  77.3 0.9 fusion.77
  78.3 0.9 fusion.77
  79.3 0.9 fusion.77
  80.2 0.9 fusion.77
  81.2 0.9 fusion.77
  82.2 0.9 fusion.77
  83.2 0.9 fusion.77
  84.1 0.9 fusion.77
  85.1 0.9 fusion.77
  86.9 2.1 convolution_convert_fusion.1
  89.1 43.7 %all-gather.6.cloned.1.call-done = bf16[4096,256]{1,0:T(8,128)(2,1)} async-done(((bf16[256,256]{1,0:T(8,128)(2,1)}), bf16[4096,256]{1,0:T(8,128)(2,1)}) %all-gather.6.cloned.1.call-update) | async-done | bytes 2097168 | tf_op jit(solution)/shard_map/all_gather | solution.py:132
  132.8 4.0 %reshape.143 = bf16[32,128,2,128]{3,2,1,0:T(2,128)(2,1)} reshape(bf16[4096,256]{1,0:T(8,128)(2,1)} %all-gather.6.cloned.1.call-done) | data formatting | bytes 4194304 | tf_op jit(solution)/shard_map/reshape | solution.py:136
  136.8 58.2 %all-gather.8.cloned.1.call-done = bf16[4096,256]{1,0:T(8,128)(2,1)} async-done(((bf16[256,256]{1,0:T(8,128)(2,1)}), bf16[4096,256]{1,0:T(8,128)(2,1)}) %all-gather.8.cloned.1.call-update) | async-done | bytes 2097168 | tf_op jit(solution)/shard_map/all_gather | solution.py:133
  195.0 4.0 %reshape.144 = bf16[32,128,2,128]{3,2,1,0:T(2,128)(2,1)} reshape(bf16[4096,256]{1,0:T(8,128)(2,1)} %all-gather.8.cloned.1.call-done) | data formatting | bytes 4194304 | tf_op jit(solution)/shard_map/reshape | solution.py:137
  199.0 141.2 %while.38 = (s32[]{:T(128)}, f32[2,128]{1,0:T(2,128)S(1)}, f32[2,128]{1,0:T(2,128)S(1)}, f32[128,2,128]{2,0,1:T(8,128)S(1)}, f32[2,128]{1,0:T(2,128)S(1)}, /*ind...) while((s32[]{:T(128)}, f32[2,128]{1,0:T(2,128)S(1)}, ...), condition=%wide.region_23.24_spmd.clone.clone, body=%wide.region_6.23_spmd.clone.clone.sunk | while | flops 34162200 | bytes 2311003 | solution.py:150
  202.3 1.0 constant_dynamic-slice_fusion.3
  207.7 1.0 constant_dynamic-slice_fusion.3
  212.6 1.0 constant_dynamic-slice_fusion.3
  216.9 1.0 constant_dynamic-slice_fusion.3
  221.3 1.0 constant_dynamic-slice_fusion.3
  225.7 1.0 constant_dynamic-slice_fusion.3
  230.0 1.0 constant_dynamic-slice_fusion.3
  234.4 1.0 constant_dynamic-slice_fusion.3
  238.7 1.0 constant_dynamic-slice_fusion.3
  243.1 1.0 constant_dynamic-slice_fusion.3
  247.5 1.0 constant_dynamic-slice_fusion.3
  251.8 1.0 constant_dynamic-slice_fusion.3
  256.2 1.0 constant_dynamic-slice_fusion.3
  260.5 1.0 constant_dynamic-slice_fusion.3
  264.9 1.0 constant_dynamic-slice_fusion.3
  269.3 1.0 constant_dynamic-slice_fusion.3
  273.6 1.0 constant_dynamic-slice_fusion.3
  278.0 1.0 constant_dynamic-slice_fusion.3
  282.4 1.0 constant_dynamic-slice_fusion.3
  286.7 1.0 constant_dynamic-slice_fusion.3
  291.1 1.0 constant_dynamic-slice_fusion.3
  295.4 1.0 constant_dynamic-slice_fusion.3
  299.8 1.0 constant_dynamic-slice_fusion.3
  304.2 1.0 constant_dynamic-slice_fusion.3
  308.5 1.0 constant_dynamic-slice_fusion.3
  312.9 1.0 constant_dynamic-slice_fusion.3
  317.2 1.0 constant_dynamic-slice_fusion.3
  321.6 1.0 constant_dynamic-slice_fusion.3
  326.0 1.0 constant_dynamic-slice_fusion.3
  330.3 1.0 constant_dynamic-slice_fusion.3
  334.7 1.0 constant_dynamic-slice_fusion.3
  339.1 1.0 constant_dynamic-slice_fusion.3
  340.4 3.6 convolution_convert_fusion
  344.1 38.5 %reduce-scatter.5.cloned.1.call-done = bf16[256,2048]{1,0:T(8,128)(2,1)} async-done(((bf16[256,4096]{1,0:T(8,128)(2,1)}), bf16[256,2048]{1,0:T(8,128)(2,1)}) %reduce-scatter.5.cloned.1.call-update) | async-done | bytes 1048592 | tf_op jit(solution)/shard_map/reduce_scatter | solution.py:173
  (337 shorter events, 33.2 us)
Async XLA Ops:
  7.2 79.8 %copy-start = (bf16[256,4096]{1,0:T(8,128)(2,1)S(1)}, bf16[256,4096]{1,0:T(8,128)(2,1)}, u32[]{:S(2)}) copy-start(bf16[256,4096]{1,0:T(8,128)(2,1)} %param.28) | copy-start | bytes 6291460
  7.2 63.3 %all-gather.10.cloned.1.call-start = ((), (), s32[]{:S(2)}) async-start(), calls=%async_computation.6 | async-start | bytes 1114112 | tf_op jit(solution)/shard_map/all_gather | solution.py:14
  10.3 75.7 %copy-start.2 = (bf16[256,256]{1,0:T(8,128)(2,1)S(1)}, bf16[256,256]{1,0:T(8,128)(2,1)}, u32[]{:S(2)}) copy-start(bf16[256,256]{1,0:T(8,128)(2,1)} %param.21) | copy-start | bytes 393220
  12.2 120.6 %all-gather.6.cloned.1.call-start = ((), (), s32[]{:S(2)}) async-start(), calls=%async_computation.3 | async-start | bytes 2228224 | tf_op jit(solution)/shard_map/all_gather | solution.py:132
  13.0 73.4 %copy-start.1 = (bf16[256,256]{1,0:T(8,128)(2,1)S(1)}, bf16[256,256]{1,0:T(8,128)(2,1)}, u32[]{:S(2)}) copy-start(bf16[256,256]{1,0:T(8,128)(2,1)} %param.23) | copy-start | bytes 393220
  13.0 182.0 %all-gather.8.cloned.1.call-start = ((), (), s32[]{:S(2)}) async-start(), calls=%async_computation.4 | async-start | bytes 2228224 | tf_op jit(solution)/shard_map/all_gather | solution.py:133
  13.7 330.4 %reduce-scatter.3.cloned.1.call-start = ((), (), s32[]{:S(2)}) async-start(), calls=%async_computation.2 | async-start | bytes 3145728 | tf_op jit(solution)/shard_map/reduce_scatter | solution.py:167
  89.0 293.5 %reduce-scatter.5.cloned.1.call-start = ((), (), s32[]{:S(2)}) async-start(), calls=%async_computation.5 | async-start | bytes 3145728 | tf_op jit(solution)/shard_map/reduce_scatter | solution.py:173
Sparse Core Ops, SparseCore 0:
  12.3 58.0 all-gather.9
  73.2 59.5 all-gather.5
  135.6 59.3 all-gather.7
  197.6 8.2 reduce-scatter.2
  344.2 38.3 reduce-scatter.4
where the time goes:
time: 393 us; the launch traced here: 389 us
  waiting for transfers between devices  150 us (38%)
  loops' own time  89.1 us (23%)
  local copies, waits for them, and re-layouts  63.5 us (16%)
  blocking collectives  43.7 us (11%)
  other arithmetic  16.9 us (4%)
  between operations  14.6 us (4%)
  matrix products  10.7 us (3%)
    another operation x1, loops' own time, softmax_heads(): carry, _ = lax.scan(inner, carry, (key_blocks, value_blocks, firsts))  85.6 us
    all_gather x1, waiting for transfers between devices, softmax_heads(): value_piece = lax.all_gather(v_soft, 'seq', axis=0, tiled=True)  58.2 us
    dynamic_slice x128, local copies, waits for them, and re-layouts, softmax_heads(): carry, _ = lax.scan(inner, carry, (key_blocks, value_blocks, firsts))  50.6 us
    all_gather x1, waiting for transfers between devices, softmax_heads(): key_piece = lax.all_gather(k_soft, 'seq', axis=0, tiled=True)  43.7 us
    unnamed x1, blocking collectives  43.7 us
    reduce_scatter x1, waiting for transfers between devices, local(): lax.psum_scatter(soft_term.astype(jnp.bfloat16).astype(jnp.float32).astyp...  38.5 us
    select_n x16, other arithmetic, turn(): return jax.tree.map(lambda a, b: jnp.where(reached, a, b), new, before)  14.9 us
    all_gather x1, waiting for transfers between devices, prefix(): lax.all_gather(part.astype(kind), axis)  8.65 us
  transfers between devices with their start and end apart: 5, of which 4 were waited for; matrix products, arithmetic and copies ran while one was open for 22% of the time, Pallas kernels for 0%

commit v1 on v0

--- a/solution.py
+++ b/solution.py
@@ -130,7 +130,12 @@
     )
     carry = start_state
     key_piece = lax.all_gather(k_soft, "seq", axis=0, tiled=True)
-    value_piece = lax.all_gather(v_soft, "seq", axis=0, tiled=True)
+    ring = [v_soft]
+    for hop in range(15):
+        ring.append(lax.ppermute(ring[-1], "seq", [(dev, (dev + 1) % 16) for dev in range(16)]))
+    value_piece = jnp.roll(
+        jnp.concatenate(ring[::-1], axis=0), (lax.axis_index("seq") + 1) * ring[0].shape[0], axis=0
+    )
     piece_rows = key_piece.shape[0]
     blocks = piece_rows // half_rows
     key_blocks = key_piece.reshape(blocks, half_rows, head_count, head_width)

time: 393 us -> 422 us (1.074)
  local copies, waits for them, and re-layouts: 63.5 us -> 81.2 us
  waiting for transfers between devices: 150 us -> 159 us
    ppermute x0 -> x15, waiting for transfers between devices: none -> 124 us  [softmax_heads(): lax.ppermute(ring[-1], 'seq', [(dev, (dev + 1) % 16) for dev in range(16)])]
    all_gather x1 -> x0, waiting for transfers between devices: 58.2 us -> none  [softmax_heads(): value_piece = lax.all_gather(v_soft, 'seq', axis=0, tiled=True)]
    all_gather x1, waiting for transfers between devices: 43.7 us -> 0.02 us  [softmax_heads(): key_piece = lax.all_gather(k_soft, 'seq', axis=0, tiled=True)]
    unnamed x12 -> x79, local copies, waits for them, and re-layouts: 1.61 us -> 17 us
    all_gather x1, waiting for transfers between devices: 8.65 us -> 0.01 us  [prefix(): lax.all_gather(part.astype(kind), axis)]
  transfers between devices with their start and end apart: 5 -> 19, of which waited for: 4 -> 15; matrix products, arithmetic and copies ran while one was open for 22% -> 25% of each run, Pallas kernels for 0% -> 0%
where the time goes in v1:
time: 422 us; the launch traced here: 418 us
  waiting for transfers between devices  159 us (38%)
  loops' own time  89 us (21%)
  local copies, waits for them, and re-layouts  81.2 us (19%)
  blocking collectives  42.5 us (10%)
  other arithmetic  16.8 us (4%)
  between operations  15.1 us (4%)
  matrix products  10.9 us (3%)
    ppermute x15, waiting for transfers between devices, softmax_heads(): lax.ppermute(ring[-1], 'seq', [(dev, (dev + 1) % 16) for dev in range(16)])  124 us
    another operation x1, loops' own time, softmax_heads(): carry, _ = lax.scan(inner, carry, (key_blocks, value_blocks, firsts))  85.7 us
    dynamic_slice x128, local copies, waits for them, and re-layouts, softmax_heads(): carry, _ = lax.scan(inner, carry, (key_blocks, value_blocks, firsts))  50.6 us
    unnamed x1, blocking collectives  42.5 us
    reduce_scatter x1, waiting for transfers between devices, local(): lax.psum_scatter(soft_term.astype(jnp.bfloat16).astype(jnp.float32).astyp...  35.5 us
    unnamed x79, local copies, waits for them, and re-layouts  17 us
    select_n x16, other arithmetic, turn(): return jax.tree.map(lambda a, b: jnp.where(reached, a, b), new, before)  14.9 us
  transfers between devices with their start and end apart: 19, of which 15 were waited for; matrix products, arithmetic and copies ran while one was open for 25% of the time, Pallas kernels for 0%

profile of v1, /device:TPU:0, one launch (start us, length us, event | category | flops | bytes accessed | tf_op | source)
XLA Modules:
  0.0 417.9 jit_solution(11037015754113246410)
XLA Ops:
  9.4 1.0 copy.69
  10.4 1.8 convolution_convert_fusion.2
  12.3 3.0 collective-permute-start
  15.3 7.7 %collective-permute-done = bf16[256,256]{1,0:T(8,128)(2,1)S(1)} collective-permute-done((bf16[256,256]{1,0:T(8,128)(2,1)}, bf16[256,256]{1,0:T(8,128)(2,1)S(1)}, u32[]{:S(2)}, u32[]{:S(2)}) %collective-permute-start) | collective-permute-done | bytes 131104 | tf_op jit(solution)/shard_map/ppermute | solution.py:135
  23.0 9.0 %collective-permute-done.1 = bf16[256,256]{1,0:T(8,128)(2,1)S(1)} collective-permute-done((bf16[256,256]{1,0:T(8,128)(2,1)S(1)}, bf16[256,256]{1,0:T(8,128)(2,1)S(1)}, u32[]{:S(2)}, u32[]{:S(2)}) %collective-permute-start.1) | collective-permute-done | bytes 131104 | tf_op jit(solution)/shard_map/ppermute | solution.py:135
  32.0 8.6 %collective-permute-done.2 = bf16[256,256]{1,0:T(8,128)(2,1)S(1)} collective-permute-done((bf16[256,256]{1,0:T(8,128)(2,1)S(1)}, bf16[256,256]{1,0:T(8,128)(2,1)S(1)}, u32[]{:S(2)}, u32[]{:S(2)}) %collective-permute-start.2) | collective-permute-done | bytes 131104 | tf_op jit(solution)/shard_map/ppermute | solution.py:135
  40.6 9.0 %collective-permute-done.3 = bf16[256,256]{1,0:T(8,128)(2,1)S(1)} collective-permute-done((bf16[256,256]{1,0:T(8,128)(2,1)S(1)}, bf16[256,256]{1,0:T(8,128)(2,1)S(1)}, u32[]{:S(2)}, u32[]{:S(2)}) %collective-permute-start.3) | collective-permute-done | bytes 131104 | tf_op jit(solution)/shard_map/ppermute | solution.py:135
  49.6 8.6 %collective-permute-done.4 = bf16[256,256]{1,0:T(8,128)(2,1)S(1)} collective-permute-done((bf16[256,256]{1,0:T(8,128)(2,1)S(1)}, bf16[256,256]{1,0:T(8,128)(2,1)S(1)}, u32[]{:S(2)}, u32[]{:S(2)}) %collective-permute-start.4) | collective-permute-done | bytes 131104 | tf_op jit(solution)/shard_map/ppermute | solution.py:135
  58.2 10.1 %collective-permute-done.5 = bf16[256,256]{1,0:T(8,128)(2,1)S(1)} collective-permute-done((bf16[256,256]{1,0:T(8,128)(2,1)S(1)}, bf16[256,256]{1,0:T(8,128)(2,1)S(1)}, u32[]{:S(2)}, u32[]{:S(2)}) %collective-permute-start.5) | collective-permute-done | bytes 131104 | tf_op jit(solution)/shard_map/ppermute | solution.py:135
  68.3 8.6 %collective-permute-done.6 = bf16[256,256]{1,0:T(8,128)(2,1)S(1)} collective-permute-done((bf16[256,256]{1,0:T(8,128)(2,1)S(1)}, bf16[256,256]{1,0:T(8,128)(2,1)S(1)}, u32[]{:S(2)}, u32[]{:S(2)}) %collective-permute-start.6) | collective-permute-done | bytes 131104 | tf_op jit(solution)/shard_map/ppermute | solution.py:135
  76.9 9.7 %collective-permute-done.7 = bf16[256,256]{1,0:T(8,128)(2,1)S(1)} collective-permute-done((bf16[256,256]{1,0:T(8,128)(2,1)S(1)}, bf16[256,256]{1,0:T(8,128)(2,1)S(1)}, u32[]{:S(2)}, u32[]{:S(2)}) %collective-permute-start.7) | collective-permute-done | bytes 131104 | tf_op jit(solution)/shard_map/ppermute | solution.py:135
  86.6 9.1 %collective-permute-done.8 = bf16[256,256]{1,0:T(8,128)(2,1)S(1)} collective-permute-done((bf16[256,256]{1,0:T(8,128)(2,1)S(1)}, bf16[256,256]{1,0:T(8,128)(2,1)S(1)}, u32[]{:S(2)}, u32[]{:S(2)}) %collective-permute-start.8) | collective-permute-done | bytes 131104 | tf_op jit(solution)/shard_map/ppermute | solution.py:135
  95.7 8.9 %collective-permute-done.9 = bf16[256,256]{1,0:T(8,128)(2,1)S(1)} collective-permute-done((bf16[256,256]{1,0:T(8,128)(2,1)S(1)}, bf16[256,256]{1,0:T(8,128)(2,1)S(1)}, u32[]{:S(2)}, u32[]{:S(2)}) %collective-permute-start.9) | collective-permute-done | bytes 131104 | tf_op jit(solution)/shard_map/ppermute | solution.py:135
  105.3 8.6 %collective-permute-done.10 = bf16[256,256]{1,0:T(8,128)(2,1)S(1)} collective-permute-done((bf16[256,256]{1,0:T(8,128)(2,1)S(1)}, bf16[256,256]{1,0:T(8,128)(2,1)S(1)}, u32[]{:S(2)}, u32[]{:S(2)}) %collective-permute-start.10) | collective-permute-done | bytes 131104 | tf_op jit(solution)/shard_map/ppermute | solution.py:135
  114.5 8.6 %collective-permute-done.11 = bf16[256,256]{1,0:T(8,128)(2,1)S(1)} collective-permute-done((bf16[256,256]{1,0:T(8,128)(2,1)S(1)}, bf16[256,256]{1,0:T(8,128)(2,1)S(1)}, u32[]{:S(2)}, u32[]{:S(2)}) %collective-permute-start.11) | collective-permute-done | bytes 131104 | tf_op jit(solution)/shard_map/ppermute | solution.py:135
  123.2 8.6 %collective-permute-done.12 = bf16[256,256]{1,0:T(8,128)(2,1)} collective-permute-done((bf16[256,256]{1,0:T(8,128)(2,1)S(1)}, bf16[256,256]{1,0:T(8,128)(2,1)}, u32[]{:S(2)}, u32[]{:S(2)}) %collective-permute-start.12) | collective-permute-done | bytes 131104 | tf_op jit(solution)/shard_map/ppermute | solution.py:135
  131.8 1.2 convolution_multiply_fusion.4
  133.0 8.8 %collective-permute-done.13 = bf16[256,256]{1,0:T(8,128)(2,1)} collective-permute-done((bf16[256,256]{1,0:T(8,128)(2,1)}, bf16[256,256]{1,0:T(8,128)(2,1)}, u32[]{:S(2)}, u32[]{:S(2)}) %collective-permute-start.13) | collective-permute-done | bytes 131104 | tf_op jit(solution)/shard_map/ppermute | solution.py:135
  141.8 1.6 reshape.130
  144.3 1.2 dynamic-slice
  146.5 42.5 %all-reduce = bf16[32]{0:T(256)(128)(2,1)S(1)} all-reduce(bf16[32]{0:T(256)(128)(2,1)S(1)} %dynamic-update-slice), channel_id=2, replica_groups=mesh['seq'=16,'head'=2] {'seq'}, use_global_device_ids=true, to_apply=%add | all-reduce | flops 32 | bytes 128
  189.2 1.1 constant_dynamic-update-slice_fusion.31
  202.6 1.5 constant_dynamic-slice_fusion.2
  204.1 4.0 reshape.144
  208.1 15.5 %while.39 = (s32[]{:T(128)}, f32[2,128,128]{2,1,0:T(8,128)S(1)}, s32[]{:T(128)}, bf16[16,2]{1,0:T(8,128)(2,1)S(1)}, bf16[16,2,128,128]{3,2,1,0:T(8,128)(2,1)}, /*index=5*/s32[]{:T(128)}, s32[]{:T(128)}) while((s32[]{:T(128)}, f32[2,128,128]{2,1,0:T(8,128)S(1)}, s32[]{:T(128)}, bf16[16,2]{1,0:T(8,128)(2,1)S(1)}, ...), condition=%wide.region_3.4_spmd.clone, body=%wide.region_2.3_spmd.clone.sunk | while | flops 163846 | bytes 327805 | solution.py:31
  209.1 0.9 fusion.77
  210.1 0.9 fusion.77
  224.5 2.1 convolution_convert_fusion.1
  226.7 4.1 reshape.143
  230.8 141.1 %while.38 = (s32[]{:T(128)}, f32[2,128]{1,0:T(2,128)S(1)}, f32[2,128]{1,0:T(2,128)S(1)}, f32[128,2,128]{2,0,1:T(8,128)S(1)}, f32[2,128]{1,0:T(2,128)S(1)}, /*ind...) while((s32[]{:T(128)}, f32[2,128]{1,0:T(2,128)S(1)}, ...), condition=%wide.region_23.24_spmd.clone.clone, body=%wide.region_6.23_spmd.clone.clone.sunk | while | flops 34162200 | bytes 2310995 | solution.py:155
  234.1 1.0 constant_dynamic-slice_fusion.4
  239.5 1.0 constant_dynamic-slice_fusion.4
  244.4 1.0 constant_dynamic-slice_fusion.4
  248.7 1.0 constant_dynamic-slice_fusion.4
  253.1 1.0 constant_dynamic-slice_fusion.4
  257.4 1.0 constant_dynamic-slice_fusion.4
  261.8 1.0 constant_dynamic-slice_fusion.4
  266.2 1.0 constant_dynamic-slice_fusion.4
  270.5 1.0 constant_dynamic-slice_fusion.4
  274.9 1.0 constant_dynamic-slice_fusion.4
  279.2 1.0 constant_dynamic-slice_fusion.4
  283.6 1.0 constant_dynamic-slice_fusion.4
  288.0 1.0 constant_dynamic-slice_fusion.4
  292.3 1.0 constant_dynamic-slice_fusion.4
  296.7 1.0 constant_dynamic-slice_fusion.4
  301.0 1.0 constant_dynamic-slice_fusion.4
  305.4 1.0 constant_dynamic-slice_fusion.4
  309.8 1.0 constant_dynamic-slice_fusion.4
  314.1 1.0 constant_dynamic-slice_fusion.4
  318.5 1.0 constant_dynamic-slice_fusion.4
  322.8 1.0 constant_dynamic-slice_fusion.4
  327.2 1.0 constant_dynamic-slice_fusion.4
  331.6 1.0 constant_dynamic-slice_fusion.4
  335.9 1.0 constant_dynamic-slice_fusion.4
  340.3 1.0 constant_dynamic-slice_fusion.4
  344.6 1.0 constant_dynamic-slice_fusion.4
  349.0 1.0 constant_dynamic-slice_fusion.4
  353.4 1.0 constant_dynamic-slice_fusion.4
  357.7 1.0 constant_dynamic-slice_fusion.4
  362.1 1.0 constant_dynamic-slice_fusion.4
  366.4 1.0 constant_dynamic-slice_fusion.4
  370.8 1.0 constant_dynamic-slice_fusion.4
  372.2 3.7 convolution_convert_fusion
  375.9 35.5 %reduce-scatter.5.cloned.1.call-done = bf16[256,2048]{1,0:T(8,128)(2,1)} async-done(((bf16[256,4096]{1,0:T(8,128)(2,1)}), bf16[256,2048]{1,0:T(8,128)(2,1)}) %reduce-scatter.5.cloned.1.call-update) | async-done | bytes 1048592 | tf_op jit(solution)/shard_map/reduce_scatter | solution.py:178
  (433 shorter events, 59.2 us)
Async XLA Ops:
  7.2 217.3 %copy-start = (bf16[256,4096]{1,0:T(8,128)(2,1)S(1)}, bf16[256,4096]{1,0:T(8,128)(2,1)}, u32[]{:S(2)}) copy-start(bf16[256,4096]{1,0:T(8,128)(2,1)} %param.28) | copy-start | bytes 6291460
  7.2 192.3 %copy-start.2 = (bf16[256,256]{1,0:T(8,128)(2,1)S(1)}, bf16[256,256]{1,0:T(8,128)(2,1)}, u32[]{:S(2)}) copy-start(bf16[256,256]{1,0:T(8,128)(2,1)} %param.27) | copy-start | bytes 393220
  7.2 200.9 %all-gather.7.cloned.1.call-start = ((), (), s32[]{:S(2)}) async-start(), calls=%async_computation.5 | async-start | bytes 1114112 | tf_op jit(solution)/shard_map/all_gather | solution.py:14
  10.4 30.2 %copy-start.19 = (bf16[256,256]{0,1:T(8,128)(2,1)}, bf16[256,256]{0,1:T(8,128)(2,1)S(1)}, u32[]{:S(2)}) copy-start(bf16[256,256]{0,1:T(8,128)(2,1)S(1)} %copy.69) | copy-start | bytes 393220
  12.2 214.4 %all-gather.5.cloned.1.call-start = ((), (), s32[]{:S(2)}) async-start(), calls=%async_computation.3 | async-start | bytes 2228224 | tf_op jit(solution)/shard_map/all_gather | solution.py:132
  12.3 10.7 %collective-permute-start = (bf16[256,256]{1,0:T(8,128)(2,1)}, bf16[256,256]{1,0:T(8,128)(2,1)S(1)}, u32[]{:S(2)}, u32[]{:S(2)}) collective-permute-start(bf16[256,256]{1,0:T(8,128)(2,1)} %param.27), channel_id=1, source_target_pairs={{0,2},{2,4},{4,6},{6,8},{8,10},{10,12},{12,14},{14,16},{16,18},{18... | collective-permute-start | bytes 393224 | tf_op jit(solution)/shard_map/ppermute | solution.py:135
  23.0 9.0 %collective-permute-start.1 = (bf16[256,256]{1,0:T(8,128)(2,1)S(1)}, bf16[256,256]{1,0:T(8,128)(2,1)S(1)}, u32[]{:S(2)}, u32[]{:S(2)}) collective-permute-start(bf16[256,256]{1,0:T(8,128)(2,1)S(1)} %collective-permute-done), channel_id=1, source_target_pairs={{0,2},{2,4},{4,6},{6,8},{8,10},{10,12},{12,14},{14,16},{16,18},{18... | collective-permute-start | bytes 393224 | tf_op jit(solution)/shard_map/ppermute | solution.py:135
  32.0 8.6 %collective-permute-start.2 = (bf16[256,256]{1,0:T(8,128)(2,1)S(1)}, bf16[256,256]{1,0:T(8,128)(2,1)S(1)}, u32[]{:S(2)}, u32[]{:S(2)}) collective-permute-start(bf16[256,256]{1,0:T(8,128)(2,1)S(1)} %collective-permute-done.1), channel_id=1, source_target_pairs={{0,2},{2,4},{4,6},{6,8},{8,10},{10,12},{12,14},{14,16},{16,18},{18... | collective-permute-start | bytes 393224 | tf_op jit(solution)/shard_map/ppermute | solution.py:135
  40.6 9.0 %collective-permute-start.3 = (bf16[256,256]{1,0:T(8,128)(2,1)S(1)}, bf16[256,256]{1,0:T(8,128)(2,1)S(1)}, u32[]{:S(2)}, u32[]{:S(2)}) collective-permute-start(bf16[256,256]{1,0:T(8,128)(2,1)S(1)} %collective-permute-done.2), channel_id=1, source_target_pairs={{0,2},{2,4},{4,6},{6,8},{8,10},{10,12},{12,14},{14,16},{16,18},{18... | collective-permute-start | bytes 393224 | tf_op jit(solution)/shard_map/ppermute | solution.py:135
  49.6 8.6 %collective-permute-start.4 = (bf16[256,256]{1,0:T(8,128)(2,1)S(1)}, bf16[256,256]{1,0:T(8,128)(2,1)S(1)}, u32[]{:S(2)}, u32[]{:S(2)}) collective-permute-start(bf16[256,256]{1,0:T(8,128)(2,1)S(1)} %collective-permute-done.3), channel_id=1, source_target_pairs={{0,2},{2,4},{4,6},{6,8},{8,10},{10,12},{12,14},{14,16},{16,18},{18... | collective-permute-start | bytes 393224 | tf_op jit(solution)/shard_map/ppermute | solution.py:135
  58.1 83.7 %copy-start.3 = (bf16[256,256]{1,0:T(8,128)(2,1)}, bf16[256,256]{1,0:T(8,128)(2,1)S(1)}, u32[]{:S(2)}) copy-start(bf16[256,256]{1,0:T(8,128)(2,1)S(1)} %collective-permute-done.4) | copy-start | bytes 393220
  58.2 10.1 %collective-permute-start.5 = (bf16[256,256]{1,0:T(8,128)(2,1)S(1)}, bf16[256,256]{1,0:T(8,128)(2,1)S(1)}, u32[]{:S(2)}, u32[]{:S(2)}) collective-permute-start(bf16[256,256]{1,0:T(8,128)(2,1)S(1)} %collective-permute-done.4), channel_id=1, source_target_pairs={{0,2},{2,4},{4,6},{6,8},{8,10},{10,12},{12,14},{14,16},{16,18},{18... | collective-permute-start | bytes 393224 | tf_op jit(solution)/shard_map/ppermute | solution.py:135
  68.3 63.4 %copy-start.5 = (bf16[256,256]{1,0:T(8,128)(2,1)}, bf16[256,256]{1,0:T(8,128)(2,1)S(1)}, u32[]{:S(2)}) copy-start(bf16[256,256]{1,0:T(8,128)(2,1)S(1)} %collective-permute-done.5) | copy-start | bytes 393220
  68.3 8.6 %collective-permute-start.6 = (bf16[256,256]{1,0:T(8,128)(2,1)S(1)}, bf16[256,256]{1,0:T(8,128)(2,1)S(1)}, u32[]{:S(2)}, u32[]{:S(2)}) collective-permute-start(bf16[256,256]{1,0:T(8,128)(2,1)S(1)} %collective-permute-done.5), channel_id=1, source_target_pairs={{0,2},{2,4},{4,6},{6,8},{8,10},{10,12},{12,14},{14,16},{16,18},{18... | collective-permute-start | bytes 393224 | tf_op jit(solution)/shard_map/ppermute | solution.py:135
  76.9 54.9 %copy-start.7 = (bf16[256,256]{1,0:T(8,128)(2,1)}, bf16[256,256]{1,0:T(8,128)(2,1)S(1)}, u32[]{:S(2)}) copy-start(bf16[256,256]{1,0:T(8,128)(2,1)S(1)} %collective-permute-done.6) | copy-start | bytes 393220
  76.9 9.7 %collective-permute-start.7 = (bf16[256,256]{1,0:T(8,128)(2,1)S(1)}, bf16[256,256]{1,0:T(8,128)(2,1)S(1)}, u32[]{:S(2)}, u32[]{:S(2)}) collective-permute-start(bf16[256,256]{1,0:T(8,128)(2,1)S(1)} %collective-permute-done.6), channel_id=1, source_target_pairs={{0,2},{2,4},{4,6},{6,8},{8,10},{10,12},{12,14},{14,16},{16,18},{18... | collective-permute-start | bytes 393224 | tf_op jit(solution)/shard_map/ppermute | solution.py:135
  86.6 45.2 %copy-start.9 = (bf16[256,256]{1,0:T(8,128)(2,1)}, bf16[256,256]{1,0:T(8,128)(2,1)S(1)}, u32[]{:S(2)}) copy-start(bf16[256,256]{1,0:T(8,128)(2,1)S(1)} %collective-permute-done.7) | copy-start | bytes 393220
  86.6 9.1 %collective-permute-start.8 = (bf16[256,256]{1,0:T(8,128)(2,1)S(1)}, bf16[256,256]{1,0:T(8,128)(2,1)S(1)}, u32[]{:S(2)}, u32[]{:S(2)}) collective-permute-start(bf16[256,256]{1,0:T(8,128)(2,1)S(1)} %collective-permute-done.7), channel_id=1, source_target_pairs={{0,2},{2,4},{4,6},{6,8},{8,10},{10,12},{12,14},{14,16},{16,18},{18... | collective-permute-start | bytes 393224 | tf_op jit(solution)/shard_map/ppermute | solution.py:135
  95.7 36.0 %copy-start.11 = (bf16[256,256]{1,0:T(8,128)(2,1)}, bf16[256,256]{1,0:T(8,128)(2,1)S(1)}, u32[]{:S(2)}) copy-start(bf16[256,256]{1,0:T(8,128)(2,1)S(1)} %collective-permute-done.8) | copy-start | bytes 393220
  95.7 8.9 %collective-permute-start.9 = (bf16[256,256]{1,0:T(8,128)(2,1)S(1)}, bf16[256,256]{1,0:T(8,128)(2,1)S(1)}, u32[]{:S(2)}, u32[]{:S(2)}) collective-permute-start(bf16[256,256]{1,0:T(8,128)(2,1)S(1)} %collective-permute-done.8), channel_id=1, source_target_pairs={{0,2},{2,4},{4,6},{6,8},{8,10},{10,12},{12,14},{14,16},{16,18},{18... | collective-permute-start | bytes 393224 | tf_op jit(solution)/shard_map/ppermute | solution.py:135
  104.6 0.6 copy-start.13
  105.3 8.6 %collective-permute-start.10 = (bf16[256,256]{1,0:T(8,128)(2,1)S(1)}, bf16[256,256]{1,0:T(8,128)(2,1)S(1)}, u32[]{:S(2)}, u32[]{:S(2)}) collective-permute-start(bf16[256,256]{1,0:T(8,128)(2,1)S(1)} %collective-permute-done.9), channel_id=1, source_target_pairs={{0,2},{2,4},{4,6},{6,8},{8,10},{10,12},{12,14},{14,16},{16,18},{18... | collective-permute-start | bytes 393224 | tf_op jit(solution)/shard_map/ppermute | solution.py:135
  113.8 0.7 copy-start.15
  114.5 8.6 %collective-permute-start.11 = (bf16[256,256]{1,0:T(8,128)(2,1)S(1)}, bf16[256,256]{1,0:T(8,128)(2,1)S(1)}, u32[]{:S(2)}, u32[]{:S(2)}) collective-permute-start(bf16[256,256]{1,0:T(8,128)(2,1)S(1)} %collective-permute-done.10), channel_id=1, source_target_pairs={{0,2},{2,4},{4,6},{6,8},{8,10},{10,12},{12,14},{14,16},{16,18},{18... | collective-permute-start | bytes 393224 | tf_op jit(solution)/shard_map/ppermute | solution.py:135
  123.0 18.7 %copy-start.17 = (bf16[256,256]{1,0:T(8,128)(2,1)}, bf16[256,256]{1,0:T(8,128)(2,1)S(1)}, u32[]{:S(2)}) copy-start(bf16[256,256]{1,0:T(8,128)(2,1)S(1)} %collective-permute-done.11) | copy-start | bytes 393220
  123.0 8.7 %collective-permute-start.12 = (bf16[256,256]{1,0:T(8,128)(2,1)S(1)}, bf16[256,256]{1,0:T(8,128)(2,1)}, u32[]{:S(2)}, u32[]{:S(2)}) collective-permute-start(bf16[256,256]{1,0:T(8,128)(2,1)S(1)} %collective-permute-done.11), channel_id=1, source_target_pairs={{0,2},{2,4},{4,6},{6,8},{8,10},{10,12},{12,14},{14,16},{16,18},{18... | collective-permute-start | bytes 393224 | tf_op jit(solution)/shard_map/ppermute | solution.py:135
  123.1 252.8 %reduce-scatter.3.cloned.1.call-start = ((), (), s32[]{:S(2)}) async-start(), calls=%async_computation.2 | async-start | bytes 3145728 | tf_op jit(solution)/shard_map/reduce_scatter | solution.py:172
  131.7 10.0 %collective-permute-start.13 = (bf16[256,256]{1,0:T(8,128)(2,1)}, bf16[256,256]{1,0:T(8,128)(2,1)}, u32[]{:S(2)}, u32[]{:S(2)}) collective-permute-start(bf16[256,256]{1,0:T(8,128)(2,1)} %collective-permute-done.12), channel_id=1, source_target_pairs={{0,2},{2,4},{4,6},{6,8},{8,10},{10,12},{12,14},{14,16},{16,18},{18... | collective-permute-start | bytes 393224 | tf_op jit(solution)/shard_map/ppermute | solution.py:135
  141.8 47.4 %collective-permute-start.14 = (bf16[256,256]{1,0:T(8,128)(2,1)}, bf16[256,256]{1,0:T(8,128)(2,1)}, u32[]{:S(2)}, u32[]{:S(2)}) collective-permute-start(bf16[256,256]{1,0:T(8,128)(2,1)} %collective-permute-done.13), channel_id=1, source_target_pairs={{0,2},{2,4},{4,6},{6,8},{8,10},{10,12},{12,14},{14,16},{16,18},{18... | collective-permute-start | bytes 393224 | tf_op jit(solution)/shard_map/ppermute | solution.py:135
  189.1 13.2 %copy-start.18 = (bf16[256,256]{1,0:T(8,128)(2,1)S(1)}, bf16[256,256]{1,0:T(8,128)(2,1)}, u32[]{:S(2)}) copy-start(bf16[256,256]{1,0:T(8,128)(2,1)} %copy-done.17) | copy-start | bytes 393220
  189.1 13.2 %copy-start.16 = (bf16[256,256]{1,0:T(8,128)(2,1)S(1)}, bf16[256,256]{1,0:T(8,128)(2,1)}, u32[]{:S(2)}) copy-start(bf16[256,256]{1,0:T(8,128)(2,1)} %copy-done.15) | copy-start | bytes 393220
  189.1 13.2 %copy-start.14 = (bf16[256,256]{1,0:T(8,128)(2,1)S(1)}, bf16[256,256]{1,0:T(8,128)(2,1)}, u32[]{:S(2)}) copy-start(bf16[256,256]{1,0:T(8,128)(2,1)} %copy-done.13) | copy-start | bytes 393220
  189.1 13.3 %copy-start.12 = (bf16[256,256]{1,0:T(8,128)(2,1)S(1)}, bf16[256,256]{1,0:T(8,128)(2,1)}, u32[]{:S(2)}) copy-start(bf16[256,256]{1,0:T(8,128)(2,1)} %copy-done.11) | copy-start | bytes 393220
  189.1 13.3 %copy-start.10 = (bf16[256,256]{1,0:T(8,128)(2,1)S(1)}, bf16[256,256]{1,0:T(8,128)(2,1)}, u32[]{:S(2)}) copy-start(bf16[256,256]{1,0:T(8,128)(2,1)} %copy-done.9) | copy-start | bytes 393220
  189.1 13.3 %copy-start.8 = (bf16[256,256]{1,0:T(8,128)(2,1)S(1)}, bf16[256,256]{1,0:T(8,128)(2,1)}, u32[]{:S(2)}) copy-start(bf16[256,256]{1,0:T(8,128)(2,1)} %copy-done.7) | copy-start | bytes 393220
  189.1 13.3 %copy-start.6 = (bf16[256,256]{1,0:T(8,128)(2,1)S(1)}, bf16[256,256]{1,0:T(8,128)(2,1)}, u32[]{:S(2)}) copy-start(bf16[256,256]{1,0:T(8,128)(2,1)} %copy-done.5) | copy-start | bytes 393220
  189.1 13.3 %copy-start.4 = (bf16[256,256]{1,0:T(8,128)(2,1)S(1)}, bf16[256,256]{1,0:T(8,128)(2,1)}, u32[]{:S(2)}) copy-start(bf16[256,256]{1,0:T(8,128)(2,1)} %copy-done.3) | copy-start | bytes 393220
  202.6 21.1 %copy-start.20 = (bf16[256,256]{1,0:T(8,128)(2,1)S(1)}, bf16[256,256]{1,0:T(8,128)(2,1)}, u32[]{:S(2)}) copy-start(bf16[256,256]{1,0:T(8,128)(2,1)} %param.21) | copy-start | bytes 393220
  204.1 19.9 %copy-start.1 = (bf16[256,256]{1,0:T(8,128)(2,1)S(1)}, bf16[256,256]{1,0:T(8,128)(2,1)}, u32[]{:S(2)}) copy-start(bf16[256,256]{1,0:T(8,128)(2,1)} %param.23) | copy-start | bytes 393220
  226.6 184.8 %reduce-scatter.5.cloned.1.call-start = ((), (), s32[]{:S(2)}) async-start(), calls=%async_computation.4 | async-start | bytes 3145728 | tf_op jit(solution)/shard_map/reduce_scatter | solution.py:178
Sparse Core Ops, SparseCore 0:
  12.4 60.8 all-gather.6
  123.2 63.0 all-gather.4
  226.8 5.4 reduce-scatter.2
  376.0 35.3 reduce-scatter.4
